TPU v7x, 32 devices: a whole 2x2x4 slice. The times are simulated.
32 devices in a mesh: groups: 2 (over x), coarse: 16 (over z, y, core).
Axes of the slice: x: 2, y: 2, z: 4, core: 2. Of those that a mesh axis runs over, the one named last changes fastest.
Arguments:
- fine_feats: bfloat16 [49152, 256], P(('groups', 'coarse')), parts along dimension 0, may hold values from -60 to 60
- down_weight: bfloat16 [8, 256, 512], replicated, may hold values from -0.125 to 0.125
- gain: float32 [512], replicated, may hold values from 0.1 to 1.9
- shift: float32 [512], replicated, may hold values from -1 to 1
- subm_weight: bfloat16 [27, 512, 256], replicated, may hold values from -0.078125 to 0.078125
- child: int32 [16, 6144], P('groups', 'coarse'), parts along dimension 0, may hold values from 0 to 1536, as said below
- live: int32 [32], P(('groups', 'coarse')), parts along dimension 0, may hold values from 128 to 384, as said below
- send_rows: int32 [8, 1024], P('groups', 'coarse'), parts along dimension 0, may hold values from 0 to 383, as said below
- nbr: int32 [54, 6144], P('groups', 'coarse'), parts along dimension 0, may hold values from 0 to 640, as said below
- grad_out: bfloat16 [12288, 256], P(('groups', 'coarse')), parts along dimension 0, may hold values from -8 to 8
Outputs:
- features_out: bfloat16 [12288, 256], P(('groups', 'coarse')), parts along dimension 0
- grad_fine: bfloat16 [49152, 256], P(('groups', 'coarse')), parts along dimension 0
- grad_down: bfloat16 [16, 256, 512], P('groups'), parts along dimension 0
- grad_gain: float32 [1024], P('groups'), parts along dimension 0
- grad_shift: float32 [1024], P('groups'), parts along dimension 0
There are 2 independent parts, one for each index of `groups`. A program takes and returns all parts, laid end to end along the dimension named above; an argument that names none is the same for every part. Nothing has to cross between parts.
Inputs may be any that keep to these rules, and one draw needn't show every extreme that they name: Within each block, every fine row 0..1535 is the child of exactly one (k, p); 1536 marks a missing child. `live`: some block is full in every draw. `send_rows`: entry [j, b*64 + i] is a local row of block b. `nbr`: indexes the table of the row's own block; entry 640 is the zero row and occurs; entry k = 13 is the row itself.
All inputs are finite; a program needn't handle non-finite values.
Results may differ from a plain program's by a relative error of at most 0.0059.
Values may be sent and summed in bfloat16 or wider, within the bound.
A program may use at most 128 MiB of HBM per device.

v0:
```python
import jax
import jax.numpy as jnp
from jax import lax
from jax.sharding import PartitionSpec as P

OFFSETS = (1, 2, -1, -2)
EPSILON = 1e-05


def shifted(block, axis, distance):
    devices = range(lax.axis_size(axis))
    route = [(i - distance, i) for i in devices if i - distance in devices]
    return lax.ppermute(block, axis, route)


def silu_parts(hidden):
    sigmoid_v = 1.0 / (1.0 + jnp.exp(-hidden))
    return (hidden * sigmoid_v, sigmoid_v * (1.0 + hidden * (1.0 - sigmoid_v)))


def body(fine_feats, down_weight, gain, shift, subm_weight, child, live, send_rows, nbr, grad_out):
    fine_rows, channels_in = fine_feats.shape
    slots_down, coarse_rows = child.shape
    offsets_subm = nbr.shape[0]
    channels = down_weight.shape[2]
    width_out = subm_weight.shape[2]
    directions, halo_rows = send_rows.shape
    fine_table = jnp.concatenate([fine_feats, jnp.zeros((1, channels_in), jnp.bfloat16)], 0)
    gathered = fine_table[child.T].reshape(coarse_rows, slots_down * channels_in)
    flat_down = down_weight.reshape(slots_down * channels_in, channels)
    conv_out = jnp.dot(gathered, flat_down, preferred_element_type=jnp.float32).astype(jnp.bfloat16)
    conv_wide = lax.optimization_barrier(conv_out).astype(jnp.float32)
    row_mask = (lax.iota(jnp.int32, coarse_rows) < live[0]).astype(jnp.float32)[:, None]
    live_count = jnp.sum(live.astype(jnp.float32))
    masked = row_mask * conv_wide
    column_sum, square_sum, filled = lax.psum(
        (jnp.sum(masked, 0), jnp.sum(masked * conv_wide, 0), live_count), "coarse"
    )
    mean_row = column_sum / filled
    variance = square_sum / filled - mean_row * mean_row
    inv_std = lax.rsqrt(variance + EPSILON)
    normed = (conv_wide - mean_row) * inv_std
    hidden = normed * gain + shift
    activated, silu_slope = silu_parts(hidden)
    active = (row_mask * activated).astype(jnp.bfloat16)
    outgoing = active[send_rows]
    received = jnp.stack(
        [shifted(outgoing[slot_j], "coarse", offset) for slot_j, offset in enumerate(OFFSETS)]
    )
    table_ext = jnp.concatenate(
        [
            active,
            received.reshape(directions * halo_rows, channels),
            jnp.zeros((1, channels), jnp.bfloat16),
        ],
        0,
    )
    conv_in = table_ext[nbr.T].reshape(coarse_rows, offsets_subm * channels)
    flat_subm = subm_weight.reshape(offsets_subm * channels, width_out)
    features_out = jnp.dot(conv_in, flat_subm, preferred_element_type=jnp.float32).astype(
        jnp.bfloat16
    )
    spread_grad = lax.dot_general(
        grad_out, flat_subm, (((1,), (1,)), ((), ())), preferred_element_type=jnp.float32
    )
    table_grad = (
        jnp.zeros((table_ext.shape[0], channels), jnp.float32)
        .at[nbr.T.reshape(-1)]
        .add(spread_grad.reshape(coarse_rows * offsets_subm, channels))
    )
    own_grad = table_grad[:coarse_rows]
    back_grad = table_grad[coarse_rows : coarse_rows + directions * halo_rows].reshape(
        directions, halo_rows, channels
    )
    returned = jnp.stack(
        [shifted(back_grad[slot_j], "coarse", -offset) for slot_j, offset in enumerate(OFFSETS)]
    )
    grad_active = own_grad.at[send_rows.reshape(-1)].add(
        returned.reshape(directions * halo_rows, channels)
    )
    grad_hidden = row_mask * grad_active * silu_slope
    grad_gain, grad_shift = lax.psum(
        (jnp.sum(grad_hidden * normed, 0), jnp.sum(grad_hidden, 0)), "coarse"
    )
    grad_pre = (
        row_mask * gain * inv_std * (grad_hidden - (grad_shift + normed * grad_gain) / filled)
    ).astype(jnp.bfloat16)
    spread_down = lax.dot_general(
        grad_pre, flat_down, (((1,), (1,)), ((), ())), preferred_element_type=jnp.float32
    )
    fine_grad = (
        jnp.zeros((fine_rows + 1, channels_in), jnp.float32)
        .at[child.T.reshape(-1)]
        .add(spread_down.reshape(coarse_rows * slots_down, channels_in))
    )
    grad_fine = fine_grad[:fine_rows].astype(jnp.bfloat16)
    weight_term = lax.dot_general(
        gathered, grad_pre, (((0,), (0,)), ((), ())), preferred_element_type=jnp.float32
    )
    grad_down = lax.psum(weight_term, "coarse").astype(jnp.bfloat16)
    return (
        features_out,
        grad_fine,
        grad_down.reshape(slots_down, channels_in, channels),
        grad_gain,
        grad_shift,
    )


def solution(mesh):
    in_specs = (
        P(("groups", "coarse"), None),
        P(),
        P(),
        P(),
        P(),
        P("groups", "coarse"),
        P(("groups", "coarse")),
        P("groups", "coarse"),
        P("groups", "coarse"),
        P(("groups", "coarse"), None),
    )
    out_specs = (
        P(("groups", "coarse"), None),
        P(("groups", "coarse"), None),
        P("groups", None, None),
        P("groups"),
        P("groups"),
    )
    return jax.shard_map(body, mesh=mesh, in_specs=in_specs, out_specs=out_specs, check_vma=False)
```

profile of v0, /device:TPU:0, one launch (start us, length us, event | category | flops | bytes accessed | tf_op | source)
XLA Modules:
  0.0 410.6 jit_solution(9187957465798868985)
XLA Ops:
  0.6 0.0 copy-start
  0.6 13.3 %fusion.54 = f32[384,13824]{1,0:T(8,128)} fusion(bf16[384,256]{1,0:T(8,128)(2,1)} %param.19, bf16[13824,256]{1,0:T(8,128)(2,1)} %bitcast.39), kind=kOutput, calls=%fused_computation.69 | convolution fusion | flops 2717908992 | bytes 28508160 | tf_op jit(solution)/shard_map/dot_general | solution.py:63
  13.9 21.6 %reshape.188 = f32[10368,512]{1,0:T(8,128)} reshape(f32[384,13824]{1,0:T(8,128)} %fusion.54) | data formatting | bytes 42467328 | tf_op jit(solution)/shard_map/reshape | solution.py:69
  35.5 0.1 copy.22
  35.7 0.2 reshape.151
  35.9 0.1 fusion.44
  36.1 64.4 %scatter_custom_fusion = f32[641,512]{1,0:T(8,128)S(1)} fusion(s32[10368]{0:T(1024)S(1)} %fusion.44, f32[10368,512]{1,0:T(8,128)} %reshape.188, f32[]{:T(128)} %constant.11.clone.1), kind=kCustom, calls=%fused_computation.45 | custom fusion | flops 5308416 | bytes 1313280 | tf_op jit(solution)/shard_map/scatter-add | solution.py:69
  100.5 0.8 fusion.52
  101.4 1.3 collective-permute-start.4
  102.6 1.3 collective-permute-start.5
  103.9 3.7 collective-permute-start.6
  107.6 5.5 %collective-permute-start.7 = (f32[64,512]{1,0:T(8,128)}, f32[64,512]{1,0:T(8,128)}, u32[]{:S(2)}, u32[]{:S(2)}) collective-permute-start(f32[64,512]{1,0:T(8,128)} %get-tuple-element.16), channel_id=1, source_target_pairs={{0,2},{1,3},{2,4},{3,5},{4,6},{5,7},{6,8},{7,9},{8,10},{9,11},{10,... | collective-permute-start | bytes 393224 | tf_op jit(solution)/shard_map/ppermute | solution.py:13
  113.2 0.6 reshape.154
  113.8 0.8 copy.17
  114.7 1.0 reshape.162
  115.7 1.2 concatenate.6
  116.9 13.0 %gather_fusion = bf16[3072,256]{1,0:T(8,128)(2,1)} fusion(bf16[1537,256]{1,0:T(8,128)(2,1)S(1)} %concatenate.6, s32[3072]{0:T(1024)S(1)} %broadcast_clamp_fusion), kind=kCustom, calls=%fused_computation | custom fusion | bytes 3158016 | tf_op jit(solution)/shard_map/gather | solution.py:29
  130.0 2.4 fusion.7
  133.1 0.1 copy.21
  133.2 0.1 reshape.150
  133.4 0.1 copy.19
  133.5 0.2 reshape.178
  133.7 0.2 fusion.16
  133.9 33.3 %all-reduce.2 = (f32[512]{0:T(512)S(1)}, f32[]{:T(128)}, f32[512]{0:T(512)S(1)}) all-reduce(f32[512]{0:T(512)S(1)} %get-tuple-element.8, f32[]{:T(128)} %bitcast.4, f32[512]{0:T(512)S(1)} %get-tuple-element.7), channel_id=1, replica_groups=mesh['groups'=2,'coarse'=16] {'coarse'}, use_global_device_ids=true, to_apply=%region_4.0 | all-reduce | flops 1025 | bytes 8200 | tf_op jit(solution)/shard_map/psum | solution.py:36
  167.3 0.6 broadcast_divide_fusion
  167.9 3.8 reshape.158
  171.7 0.1 reshape.170
  171.8 1.1 pad_maximum_fusion
  173.0 0.0 copy-start.8
  173.0 2.6 scatter_fusion
  175.6 2.4 fusion.50
  178.0 29.5 %all-reduce.1 = (f32[512]{0:T(512)S(1)}, f32[512]{0:T(512)S(1)}) all-reduce(f32[512]{0:T(512)S(1)} %get-tuple-element.6, f32[512]{0:T(512)S(1)} %get-tuple-element.5), channel_id=1, replica_groups=mesh['groups'=2,'coarse'=16] {'coarse'}, use_global_device_ids=true, to_apply=%region_10.0 | all-reduce | flops 1024 | bytes 8192 | tf_op jit(solution)/shard_map/psum | solution.py:82
  207.5 5.6 %fusion.46 = f32[2048,512]{1,0:T(8,128)} fusion(bf16[384,2048]{1,0:T(8,128)(2,1)} %reshape.158, f32[384,512]{1,0:T(8,128)} %get-tuple-element.14, bf16[384,512]{1,0:T(8,128)(2,1)} %copy-done.3, f32[]{:T(128)} %get-tuple-element.12, f32[512]{0:T(512)S(1)} %get-tuple-element.9, f32[512]{0:T(512)S(1)} %get-tuple-element.10, f32[512]{0:T(512)S(1)} %copy-done.8, ...), kind=kOutput, calls=%fused_computation.64 | convolution fusion | flops 807469056 | bytes 6958596 | tf_op jit(solution)/shard_map/dot_general | solution.py:97
  213.2 95.3 %all-reduce.4 = bf16[2048,512]{1,0:T(8,128)(2,1)} all-reduce(f32[2048,512]{1,0:T(8,128)} %fusion.46), channel_id=1, replica_groups=mesh['groups'=2,'coarse'=16] {'coarse'}, use_global_device_ids=true, to_apply=%region_12.0 | all-reduce | flops 1048576 | bytes 6291456 | tf_op jit(solution)/shard_map/psum | solution.py:100
  308.5 1.2 gather_fusion.1
  309.6 0.6 fusion.53
  310.3 3.6 collective-permute-start
  313.9 2.7 collective-permute-start.1
  316.6 1.3 collective-permute-start.2
  317.9 1.3 collective-permute-start.3
  319.2 4.5 %fusion.48 = f32[384,2048]{1,0:T(8,128)} fusion(bf16[2048,512]{1,0:T(8,128)(2,1)S(1)} %bitcast.38, f32[384,512]{1,0:T(8,128)} %get-tuple-element.14, bf16[384,512]{1,0:T(8,128)(2,1)S(1)} %copy-done.4, f32[]{:T(128)} %get-tuple-element.12, f32[512]{0:T(512)} %copy-done.11, f32[512]{0:T(512)} %copy-done.12, f32[512]{0:T(512)S(1)} %copy-done.8, ...), kind=kOutput, calls=%fused_computation.65 | convolution fusion | flops 807469056 | bytes 6434308 | tf_op jit(solution)/shard_map/dot_general | solution.py:88
  323.7 4.6 %reshape.204 = f32[3072,256]{1,0:T(8,128)} reshape(f32[384,2048]{1,0:T(8,128)} %fusion.48) | data formatting | bytes 6291456 | tf_op jit(solution)/shard_map/reshape | solution.py:94
  328.3 17.8 %scatter_custom_fusion.2 = f32[1537,256]{1,0:T(8,128)S(1)} fusion(s32[3072]{0:T(1024)S(1)} %bitcast.50, f32[3072,256]{1,0:T(8,128)} %reshape.204, f32[]{:T(128)} %constant.11.clone.1), kind=kCustom, calls=%fused_computation.19 | custom fusion | flops 786432 | bytes 1574400 | tf_op jit(solution)/shard_map/scatter-add | solution.py:94
  346.1 1.0 slice.71
  347.1 0.2 maximum_maximum_fusion
  347.3 29.8 %gather_fusion.2 = bf16[10368,512]{1,0:T(8,128)(2,1)} fusion(bf16[641,512]{1,0:T(8,128)(2,1)S(1)} %maximum_maximum_fusion, s32[11264]{0:T(1024)S(1)} %pad_clamp_fusion), kind=kCustom, calls=%fused_computation.2 | custom fusion | bytes 21275136 | tf_op jit(solution)/shard_map/gather | solution.py:58
  377.2 14.6 %reshape.177 = bf16[384,27,512]{2,1,0:T(8,128)(2,1)} reshape(bf16[10368,512]{1,0:T(8,128)(2,1)} %gather_fusion.2) | data formatting | bytes 21233664 | tf_op jit(solution)/shard_map/gather | solution.py:58
  391.7 18.9 %fusion.13 = bf16[384,256]{1,0:T(8,128)(2,1)} fusion(bf16[27,512,256]{2,1,0:T(8,128)(2,1)} %param.14, bf16[384,27,512]{2,1,0:T(8,128)(2,1)} %reshape.177), kind=kOutput, calls=%fused_computation.17 | convolution fusion | flops 2718007296 | bytes 17891328 | tf_op jit(solution)/shard_map/dot_general | solution.py:60
  (45 shorter events, 0.2 us)
Async XLA Ops:
  0.6 129.3 %copy-start = (bf16[8,256,512]{2,1,0:T(8,128)(2,1)S(1)}, bf16[8,256,512]{2,1,0:T(8,128)(2,1)}, u32[]{:S(2)}) copy-start(bf16[8,256,512]{2,1,0:T(8,128)(2,1)} %param.11) | copy-start | bytes 6291460
  13.9 21.6 %copy-start.5 = (s32[27,384]{1,0:T(8,128)S(1)}, s32[27,384]{1,0:T(8,128)}, u32[]{:S(2)}) copy-start(s32[27,384]{1,0:T(8,128)} %param.18) | copy-start | bytes 124420
  35.5 77.6 %copy-start.7 = (s32[4,64]{1,0:T(4,128)S(1)}, s32[4,64]{1,0:T(4,128)}, u32[]{:S(2)}) copy-start(s32[4,64]{1,0:T(4,128)} %param.17) | copy-start | bytes 3076
  35.5 78.3 %copy-start.6 = (s32[8,384]{1,0:T(8,128)S(1)}, s32[8,384]{1,0:T(8,128)}, u32[]{:S(2)}) copy-start(s32[8,384]{1,0:T(8,128)} %param.15) | copy-start | bytes 36868
  100.5 15.2 %copy-start.2 = (f32[641,512]{1,0:T(8,128)}, f32[641,512]{1,0:T(8,128)S(1)}, u32[]{:S(2)}) copy-start(f32[641,512]{1,0:T(8,128)S(1)} %scatter_custom_fusion) | copy-start | bytes 3938308
  101.4 70.5 %collective-permute-start.4 = (f32[64,512]{1,0:T(8,128)}, f32[64,512]{1,0:T(8,128)}, u32[]{:S(2)}, u32[]{:S(2)}) collective-permute-start(f32[64,512]{1,0:T(8,128)} %get-tuple-element.15), channel_id=1, source_target_pairs={{1,0},{2,1},{3,2},{4,3},{5,4},{6,5},{7,6},{8,7},{9,8},{10,9},{11,1... | collective-permute-start | bytes 393224 | tf_op jit(solution)/shard_map/ppermute | solution.py:13
  102.6 69.2 %collective-permute-start.5 = (f32[64,512]{1,0:T(8,128)}, f32[64,512]{1,0:T(8,128)}, u32[]{:S(2)}, u32[]{:S(2)}) collective-permute-start(f32[64,512]{1,0:T(8,128)} %get-tuple-element.18), channel_id=1, source_target_pairs={{2,0},{3,1},{4,2},{5,3},{6,4},{7,5},{8,6},{9,7},{10,8},{11,9},{12,... | collective-permute-start | bytes 393224 | tf_op jit(solution)/shard_map/ppermute | solution.py:13
  103.9 67.9 %collective-permute-start.6 = (f32[64,512]{1,0:T(8,128)}, f32[64,512]{1,0:T(8,128)}, u32[]{:S(2)}, u32[]{:S(2)}) collective-permute-start(f32[64,512]{1,0:T(8,128)} %get-tuple-element.17), channel_id=1, source_target_pairs={{0,1},{1,2},{2,3},{3,4},{4,5},{5,6},{6,7},{7,8},{8,9},{9,10},{10,1... | collective-permute-start | bytes 393224 | tf_op jit(solution)/shard_map/ppermute | solution.py:13
  107.6 64.2 %collective-permute-start.7 = (f32[64,512]{1,0:T(8,128)}, f32[64,512]{1,0:T(8,128)}, u32[]{:S(2)}, u32[]{:S(2)}) collective-permute-start(f32[64,512]{1,0:T(8,128)} %get-tuple-element.16), channel_id=1, source_target_pairs={{0,2},{1,3},{2,4},{3,5},{4,6},{5,7},{6,8},{7,9},{8,10},{9,11},{10,... | collective-permute-start | bytes 393224 | tf_op jit(solution)/shard_map/ppermute | solution.py:13
  130.0 37.9 %copy-start.9 = (s32[256,1]{0,1:T(1,128)S(1)}, s32[256,1]{0,1:T(1,128)}, u32[]{:S(2)}) copy-start(s32[256,1]{0,1:T(1,128)} %reshape.154) | copy-start | bytes 3076
  132.4 35.5 %copy-start.3 = (bf16[384,512]{1,0:T(8,128)(2,1)}, bf16[384,512]{1,0:T(8,128)(2,1)S(1)}, u32[]{:S(2)}) copy-start(bf16[384,512]{1,0:T(8,128)(2,1)S(1)} %fusion.7) | copy-start | bytes 1179652
  167.9 5.1 %slice-start = ((f32[641,512]{1,0:T(8,128)}), f32[384,512]{1,0:T(8,128)S(1)}, s32[]{:S(2)}) async-start(f32[641,512]{1,0:T(8,128)} %copy-done.2), calls=%async_computation | async-start | bytes 1572864 | tf_op jit(solution)/shard_map/slice | solution.py:71
  173.0 2.6 copy-start.8
  173.0 2.6 copy-start.10
  207.5 5.7 %copy-start.11 = (f32[512]{0:T(512)}, f32[512]{0:T(512)S(1)}, u32[]{:S(2)}) copy-start(f32[512]{0:T(512)S(1)} %get-tuple-element.9) | copy-start | bytes 6148
  207.5 5.7 %copy-start.12 = (f32[512]{0:T(512)}, f32[512]{0:T(512)S(1)}, u32[]{:S(2)}) copy-start(f32[512]{0:T(512)S(1)} %get-tuple-element.10) | copy-start | bytes 6148
  308.5 10.8 %copy-start.4 = (bf16[384,512]{1,0:T(8,128)(2,1)S(1)}, bf16[384,512]{1,0:T(8,128)(2,1)}, u32[]{:S(2)}) copy-start(bf16[384,512]{1,0:T(8,128)(2,1)} %copy-done.3) | copy-start | bytes 1179652
  310.3 36.8 %collective-permute-start = (bf16[64,512]{1,0:T(8,128)(2,1)}, bf16[64,512]{1,0:T(8,128)(2,1)S(1)}, u32[]{:S(2)}, u32[]{:S(2)}) collective-permute-start(bf16[64,512]{1,0:T(8,128)(2,1)} %get-tuple-element.20), channel_id=1, source_target_pairs={{0,1},{1,2},{2,3},{3,4},{4,5},{5,6},{6,7},{7,8},{8,9},{9,10},{10,1... | collective-permute-start | bytes 196616 | tf_op jit(solution)/shard_map/ppermute | solution.py:13
  313.9 33.2 %collective-permute-start.1 = (bf16[64,512]{1,0:T(8,128)(2,1)S(1)}, bf16[64,512]{1,0:T(8,128)(2,1)S(1)}, u32[]{:S(2)}, u32[]{:S(2)}) collective-permute-start(bf16[64,512]{1,0:T(8,128)(2,1)S(1)} %get-tuple-element.22), channel_id=1, source_target_pairs={{0,2},{1,3},{2,4},{3,5},{4,6},{5,7},{6,8},{7,9},{8,10},{9,11},{10,... | collective-permute-start | bytes 196616 | tf_op jit(solution)/shard_map/ppermute | solution.py:13
  316.6 30.4 %collective-permute-start.2 = (bf16[64,512]{1,0:T(8,128)(2,1)S(1)}, bf16[64,512]{1,0:T(8,128)(2,1)S(1)}, u32[]{:S(2)}, u32[]{:S(2)}) collective-permute-start(bf16[64,512]{1,0:T(8,128)(2,1)S(1)} %get-tuple-element.21), channel_id=1, source_target_pairs={{1,0},{2,1},{3,2},{4,3},{5,4},{6,5},{7,6},{8,7},{9,8},{10,9},{11,1... | collective-permute-start | bytes 196616 | tf_op jit(solution)/shard_map/ppermute | solution.py:13
  317.9 29.1 %collective-permute-start.3 = (bf16[64,512]{1,0:T(8,128)(2,1)S(1)}, bf16[64,512]{1,0:T(8,128)(2,1)S(1)}, u32[]{:S(2)}, u32[]{:S(2)}) collective-permute-start(bf16[64,512]{1,0:T(8,128)(2,1)S(1)} %get-tuple-element.23), channel_id=1, source_target_pairs={{2,0},{3,1},{4,2},{5,3},{6,4},{7,5},{8,6},{9,7},{10,8},{11,9},{12,... | collective-permute-start | bytes 196616 | tf_op jit(solution)/shard_map/ppermute | solution.py:13
  391.7 18.9 %copy-start.1 = (bf16[8,256,512]{2,1,0:T(8,128)(2,1)S(1)}, bf16[8,256,512]{2,1,0:T(8,128)(2,1)}, u32[]{:S(2)}) copy-start(bf16[8,256,512]{2,1,0:T(8,128)(2,1)} %param.11) | copy-start | bytes 6291460
where the time goes:
time: 413 us; the launch traced here: 411 us
  blocking collectives  158 us (38%)
  local copies, waits for them, and re-layouts  95.9 us (23%)
  other arithmetic  89.5 us (22%)
  matrix products  44.7 us (11%)
  starting transfers between devices  20.7 us (5%)
    psum x1, blocking collectives, body(): grad_down = lax.psum(weight_term, 'coarse').astype(jnp.bfloat16)  95.3 us
    scatter-add x1, other arithmetic, body(): table_grad = jnp.zeros((table_ext.shape[0], channels), jnp.float32).at[nb...  64.4 us
    gather x2, local copies, waits for them, and re-layouts, body(): conv_in = table_ext[nbr.T].reshape(coarse_rows, offsets_subm * channels)  44.4 us
    psum x1, blocking collectives, body(): lax.psum((jnp.sum(masked, 0), jnp.sum(masked * conv_wide, 0), live_count)...  33.3 us
    psum x1, blocking collectives, body(): lax.psum((jnp.sum(grad_hidden * normed, 0), jnp.sum(grad_hidden, 0)), 'co...  29.5 us
    reshape x1, local copies, waits for them, and re-layouts, body(): spread_grad.reshape(coarse_rows * offsets_subm, channels)  21.6 us
    ppermute x8, starting transfers between devices, shifted(): return lax.ppermute(block, axis, route)  20.7 us
    dot_general x1, matrix products, body(): jnp.dot(conv_in, flat_subm, preferred_element_type=jnp.float32)  18.9 us
  transfers between devices with their start and end apart: 8, of which 0 were waited for; matrix products, arithmetic and copies ran while one was open for 13% of the time, Pallas kernels for 0%

commit v1 on v0

v1 whole, which is shorter than its diff:
```python
import functools

import jax
import jax.numpy as jnp
from jax import lax
from jax.experimental import pallas as pl
from jax.experimental.pallas import tpu as pltpu
from jax.sharding import PartitionSpec as P

OFFSETS = (1, 2, -1, -2)
EPSILON = 1e-05
LANES = 2
F32 = jnp.float32
BF16 = jnp.bfloat16
MESH = pl.DeviceIdType.MESH


def silu_parts(hidden):
    sigmoid_v = 1.0 / (1.0 + jnp.exp(-hidden))
    return (hidden * sigmoid_v, sigmoid_v * (1.0 + hidden * (1.0 - sigmoid_v)))


def pick_rows(column, size):
    wide = lax.broadcasted_iota(jnp.int32, (column.shape[0], size), 1)
    return jnp.where(wide == column, 1.0, 0.0).astype(BF16)


def drop_rows(row, size):
    tall = lax.broadcasted_iota(jnp.int32, (size, row.shape[1]), 0)
    return jnp.where(tall == row, 1.0, 0.0).astype(BF16)


def as_column(row):
    return jnp.transpose(jnp.broadcast_to(row, (8, row.shape[1])))[:, :1]


def dot(a, b, ca=1, cb=0):
    return lax.dot_general(a, b, (((ca,), (cb,)), ((), ())), preferred_element_type=F32)


def kernel(
    n, fine, wd_hbm, gain, shift, ws_hbm, child, live, send_rows, nbr, gout,
    feat_o, fine_o, down_o, gain_o, shift_o,
    wd, ws, gath, conv, table, tgrad, facc, gpre, dspread, part,
    sbuf, rbuf, obuf, st1, st2, hsend, hrecv, bsend, brecv,
    wsem, s1s, s1r, s2s, s2r, hss, hsr, bss, bsr, rss, rsr, ags, agr,
):
    kd, cin, c = wd.shape
    ks, _, co = ws.shape
    rows = child.shape[1]
    ndir, halo = send_rows.shape
    fine_rows = fine.shape[0]
    ext = rows + ndir * halo
    q_count, total, width = part.shape
    me = lax.axis_index("coarse")

    wd_copy = pltpu.make_async_copy(wd_hbm, wd, wsem.at[0])
    ws_copy = pltpu.make_async_copy(ws_hbm, ws, wsem.at[1])
    wd_copy.start()
    ws_copy.start()

    barrier = pltpu.get_barrier_semaphore()

    @pl.loop(1, n)
    def _(d):
        pl.semaphore_signal(barrier, inc=1, device_id={"coarse": lax.rem(me + d, n)}, device_id_type=MESH)

    def remote(src, dst, ssem, rsem, to):
        return pltpu.make_async_remote_copy(
            src_ref=src, dst_ref=dst, send_sem=ssem, recv_sem=rsem,
            device_id={"coarse": to}, device_id_type=MESH,
        )

    def tell_all(st, ss, sr):
        @pl.loop(1, n)
        def _(d):
            remote(st.at[me], st.at[me], ss.at[d], sr.at[me], lax.rem(me + d, n)).start()

    def hear_all(st, ss, sr):
        @pl.loop(1, n)
        def _(d):
            src = lax.rem(me - d + n, n)
            remote(st.at[src], st.at[src], ss.at[d], sr.at[src], lax.rem(me + d, n)).wait()

    conv[...] = jnp.zeros_like(conv)
    wd_copy.wait()

    @pl.loop(0, kd)
    def _(k):
        sel = pick_rows(as_column(child[pl.ds(k, 1), :]), fine_rows)
        g = dot(sel, fine[...]).astype(BF16)
        gath[k] = g
        conv[...] += dot(g, wd[k])

    wide = conv[...].astype(BF16).astype(F32)
    conv[...] = wide
    row_mask = (lax.broadcasted_iota(jnp.int32, (rows, 1), 0) < live[0]).astype(F32)
    masked = row_mask * wide
    sums = jnp.sum(masked, 0, keepdims=True)
    squares = jnp.sum(masked * wide, 0, keepdims=True)
    pieces = c // 128
    for r in range(pieces):
        st1[me, r : r + 1, :] = sums[:, r * 128 : (r + 1) * 128]
        st1[me, pieces + r : pieces + r + 1, :] = squares[:, r * 128 : (r + 1) * 128]
    live_count = jnp.full((8, 128), live[0], jnp.int32).astype(F32)
    st1[me, 2 * pieces : 2 * pieces + 8, :] = live_count
    pl.semaphore_wait(barrier, n - 1)
    tell_all(st1, s1s, s1r)

    tgrad[...] = jnp.zeros_like(tgrad)
    ws_copy.wait()

    @pl.loop(0, ks // 3)
    def _(k3):
        total_k = None
        for i in range(3):
            k = k3 * 3 + i
            spread = dot(drop_rows(nbr[pl.ds(k, 1), :], ext), gout[...]).astype(BF16)
            term = dot(spread, ws[k], 1, 1)
            total_k = term if total_k is None else total_k + term
        tgrad[...] += total_k

    def back_copy(j):
        return remote(
            bsend.at[j], brecv.at[j], bss.at[j], bsr.at[j], lax.rem(me - OFFSETS[j] + n, n)
        )

    def halo_copy(j):
        return remote(
            hsend.at[j], hrecv.at[j], hss.at[j], hsr.at[j], lax.rem(me + OFFSETS[j] + n, n)
        )

    for j in range(ndir):
        bsend[j] = tgrad[rows + j * halo : rows + (j + 1) * halo, :].astype(BF16)
        back_copy(j).start()

    hear_all(st1, s1s, s1r)

    def add_slots(st):
        acc = st[0]
        for i in range(1, n):
            acc = acc + st[i]
        return acc

    def flat(acc, first):
        return jnp.concatenate([acc[first + r : first + r + 1, :] for r in range(pieces)], 1)

    acc1 = add_slots(st1)
    filled = acc1[2 * pieces : 2 * pieces + 1, :1]
    mean = flat(acc1, 0) / filled
    variance = flat(acc1, pieces) / filled - mean * mean
    inv_std = lax.rsqrt(variance + EPSILON)
    normed = (conv[...] - mean) * inv_std
    hidden = normed * gain[...] + shift[...]
    activated, slope = silu_parts(hidden)
    active = (row_mask * activated).astype(BF16)
    table[:rows, :] = active
    conv[...] = normed
    for j in range(ndir):
        sel = drop_rows(send_rows[j : j + 1, :], rows)
        hsend[j] = dot(sel, active, 0, 0).astype(BF16)
        halo_copy(j).start()

    grad_active = tgrad[:rows, :]
    for j in range(ndir):
        back_copy(j).wait()
        giver = me + OFFSETS[j]
        there = jnp.logical_and(giver >= 0, giver < n)
        back = jnp.where(there, brecv[j], jnp.zeros_like(brecv[j]))
        grad_active = grad_active + dot(drop_rows(send_rows[j : j + 1, :], rows), back)
    grad_hidden = row_mask * grad_active * slope
    tgrad[:rows, :] = grad_hidden
    part_gain = jnp.sum(grad_hidden * normed, 0, keepdims=True)
    part_shift = jnp.sum(grad_hidden, 0, keepdims=True)
    for r in range(pieces):
        st2[me, r : r + 1, :] = part_gain[:, r * 128 : (r + 1) * 128]
        st2[me, pieces + r : pieces + r + 1, :] = part_shift[:, r * 128 : (r + 1) * 128]
    tell_all(st2, s2s, s2r)

    for j in range(ndir):
        halo_copy(j).wait()
        giver = me - OFFSETS[j]
        there = jnp.logical_and(giver >= 0, giver < n)
        table[rows + j * halo : rows + (j + 1) * halo, :] = jnp.where(
            there, hrecv[j], jnp.zeros_like(hrecv[j])
        )
    facc[...] = jnp.zeros_like(facc)

    def forward(first, last):
        @pl.loop(first, last)
        def _(k):
            sel = pick_rows(as_column(nbr[pl.ds(k, 1), :]), ext)
            facc[...] += dot(dot(sel, table[...]).astype(BF16), ws[k])

    forward(0, 3)

    hear_all(st2, s2s, s2r)
    acc2 = add_slots(st2)
    grad_gain = flat(acc2, 0)
    grad_shift = flat(acc2, pieces)
    gain_o[...] = grad_gain
    shift_o[...] = grad_shift
    gpre[...] = (
        row_mask * gain[...] * inv_std
        * (tgrad[:rows, :] - (grad_shift + conv[...] * grad_gain) / filled)
    ).astype(BF16)

    masks = []
    while 2 ** len(masks) < n:
        masks.append(2 ** len(masks))
    steps = len(masks)
    lows, sends, partners, lengths, places = [], [], [], [], []
    low, length, place = 0, total, 0
    for m in masks:
        bit = lax.rem(me // m, 2)
        length = length // 2
        lengths.append(length)
        sends.append(pl.multiple_of(low + (1 - bit) * length, length))
        low = low + bit * length
        lows.append(pl.multiple_of(low, length))
        partners.append(me + m - 2 * m * bit)
        places.append(place)
        place += length

    def sum_copy(q, s):
        span = pl.ds(places[s], lengths[s])
        return remote(
            sbuf.at[q, span], rbuf.at[q, span], rss.at[q, s], rsr.at[q, s], partners[s]
        )

    def full_copy(q, s):
        span = pl.ds(lows[s], lengths[s])
        return remote(
            obuf.at[q, span], obuf.at[q, span], ags.at[q, s], agr.at[q, s], partners[s]
        )

    def start(q, t):
        if t < steps:
            sbuf[q, places[t] : places[t] + lengths[t], :] = part[
                q, pl.ds(sends[t], lengths[t]), :
            ].astype(BF16)
            sum_copy(q, t).start()
        elif t < 2 * steps:
            full_copy(q, 2 * steps - 1 - t).start()

    def finish(q, t):
        if t < steps:
            sum_copy(q, t).wait()
            span = pl.ds(lows[t], lengths[t])
            summed = part[q, span, :] + rbuf[q, places[t] : places[t] + lengths[t], :].astype(F32)
            if t < steps - 1:
                part[q, span, :] = summed
            else:
                obuf[q, span, :] = summed.astype(BF16)
        else:
            full_copy(q, 2 * steps - 1 - t).wait()

    for q in range(q_count):
        @pl.loop(0, kd)
        def _(k):
            part[q, pl.ds(pl.multiple_of(k * cin, cin), cin), :] = dot(
                gath[k], gpre[:, q * width : (q + 1) * width], 0, 0
            )

        start(q, 0)

    def spread_down():
        @pl.loop(0, kd)
        def _(k):
            dspread[pl.ds(pl.multiple_of(k * rows, rows), rows), :] = dot(
                gpre[...], wd[k], 1, 1
            ).astype(BF16)

    tile = 256

    def fine_tiles(first, last):
        @pl.loop(first, last)
        def _(i):
            base = pl.multiple_of(i * tile, tile)
            acc = jnp.zeros((tile, cin), F32)
            for k in range(kd):
                sel = drop_rows(child[k : k + 1, :] - base, tile)
                acc = acc + dot(sel, dspread[k * rows : (k + 1) * rows, :])
            fine_o[pl.ds(base, tile), :] = acc.astype(BF16)

    units = [functools.partial(forward, k, min(k + 2, ks)) for k in range(3, ks, 2)]
    units.append(spread_down)
    tiles = fine_rows // tile
    units += [functools.partial(fine_tiles, i, i + 1) for i in range(tiles)]
    for t in range(2 * steps):
        for q in range(q_count):
            finish(q, t)
            start(q, t + 1)
            if units:
                units.pop(0)()
    for unit in units:
        unit()
    feat_o[...] = facc[...].astype(BF16)
    for q in range(q_count):
        down_o[:, q * width : (q + 1) * width] = obuf[q]


def body(fine_feats, down_weight, gain, shift, subm_weight, child, live, send_rows, nbr, grad_out):
    n = lax.axis_size("coarse")
    fine_rows, cin = fine_feats.shape
    kd, _, c = down_weight.shape
    ks, _, co = subm_weight.shape
    rows = child.shape[1]
    ndir, halo = send_rows.shape
    ext = rows + ndir * halo
    width = c // LANES
    total = kd * cin
    steps = max(1, (n - 1).bit_length())
    slot = 2 * (c // 128)
    vmem = pl.BlockSpec(memory_space=pltpu.VMEM)
    hbm = pl.BlockSpec(memory_space=pl.ANY)
    smem = pl.BlockSpec(memory_space=pltpu.SMEM)
    dma = pltpu.SemaphoreType.DMA
    features, grad_fine, grad_down, grad_gain, grad_shift = pl.pallas_call(
        functools.partial(kernel, n),
        out_shape=(
            jax.ShapeDtypeStruct((rows, co), BF16),
            jax.ShapeDtypeStruct((fine_rows, cin), BF16),
            jax.ShapeDtypeStruct((total, c), BF16),
            jax.ShapeDtypeStruct((1, c), F32),
            jax.ShapeDtypeStruct((1, c), F32),
        ),
        in_specs=[vmem, hbm, vmem, vmem, hbm, vmem, smem, vmem, vmem, vmem],
        out_specs=(vmem,) * 5,
        scratch_shapes=[
            pltpu.VMEM((kd, cin, c), BF16),
            pltpu.VMEM((ks, c, co), BF16),
            pltpu.VMEM((kd, rows, cin), BF16),
            pltpu.VMEM((rows, c), F32),
            pltpu.VMEM((ext, c), BF16),
            pltpu.VMEM((ext, c), F32),
            pltpu.VMEM((rows, co), F32),
            pltpu.VMEM((rows, c), BF16),
            pltpu.VMEM((kd * rows, cin), BF16),
            pltpu.VMEM((LANES, total, width), F32),
            pltpu.VMEM((LANES, total, width), BF16),
            pltpu.VMEM((LANES, total, width), BF16),
            pltpu.VMEM((LANES, total, width), BF16),
            pltpu.VMEM((n, slot + 8, 128), F32),
            pltpu.VMEM((n, slot, 128), F32),
            pltpu.VMEM((ndir, halo, c), BF16),
            pltpu.VMEM((ndir, halo, c), BF16),
            pltpu.VMEM((ndir, halo, c), BF16),
            pltpu.VMEM((ndir, halo, c), BF16),
            dma((2,)),
            dma((n,)), dma((n,)), dma((n,)), dma((n,)),
            dma((ndir,)), dma((ndir,)), dma((ndir,)), dma((ndir,)),
            dma((LANES, steps)), dma((LANES, steps)), dma((LANES, steps)), dma((LANES, steps)),
        ],
        compiler_params=pltpu.CompilerParams(
            collective_id=0, has_side_effects=True, vmem_limit_bytes=56 * 1024 * 1024
        ),
    )(
        fine_feats, down_weight, gain.reshape(1, c), shift.reshape(1, c), subm_weight,
        child, live, send_rows, nbr, grad_out,
    )
    return (
        features,
        grad_fine,
        grad_down.reshape(kd, cin, c),
        grad_gain.reshape(c),
        grad_shift.reshape(c),
    )


def solution(mesh):
    in_specs = (
        P(("groups", "coarse"), None),
        P(),
        P(),
        P(),
        P(),
        P("groups", "coarse"),
        P(("groups", "coarse")),
        P("groups", "coarse"),
        P("groups", "coarse"),
        P(("groups", "coarse"), None),
    )
    out_specs = (
        P(("groups", "coarse"), None),
        P(("groups", "coarse"), None),
        P("groups", None, None),
        P("groups"),
        P("groups"),
    )
    return jax.shard_map(body, mesh=mesh, in_specs=in_specs, out_specs=out_specs, check_vma=False)
```

time: 413 us -> 107 us (0.26)
  blocking collectives: 158 us -> 0 us
  Pallas kernels: 0 us -> 97.5 us
  other arithmetic: 89.5 us -> 0 us
  local copies, waits for them, and re-layouts: 95.9 us -> 7.89 us
  matrix products: 44.7 us -> 0 us
  starting transfers between devices: 20.7 us -> 0 us
    psum x3 -> x0, blocking collectives: 158 us -> none  [the longest x1 95.3 us: body(): grad_down = lax.psum(weight_term, 'coarse').astype(jnp.bfloat16)]
    pallas_call x0 -> x1, Pallas kernels: none -> 97.5 us  [body(): pl.pallas_call(functools.partial(kernel, n), out_shape=(jax.ShapeDtypeStr...]
    scatter-add x3 -> x0, other arithmetic: 84.8 us -> none  [the longest x1 64.4 us: body(): table_grad = jnp.zeros((table_ext.shape[0], channels), jnp.float32).at[nb...]
    gather x4 -> x0, local copies, waits for them, and re-layouts: 58.6 us -> none  [the longest x2 44.4 us: body(): conv_in = table_ext[nbr.T].reshape(coarse_rows, offsets_subm * channels)]
    dot_general x5 -> x0, matrix products: 44.7 us -> none  [the longest x1 18.9 us: body(): jnp.dot(conv_in, flat_subm, preferred_element_type=jnp.float32)]
    reshape x6 -> x0, local copies, waits for them, and re-layouts: 31.1 us -> none  [the longest x1 21.6 us: body(): spread_grad.reshape(coarse_rows * offsets_subm, channels)]
    ppermute x8 -> x0, starting transfers between devices: 20.7 us -> none  [shifted(): return lax.ppermute(block, axis, route)]
    unnamed x26 -> x9, local copies, waits for them, and re-layouts: 0.06 us -> 7.89 us
  transfers between devices with their start and end apart: 8 -> 0, of which waited for: 0 -> 0; matrix products, arithmetic and copies ran while one was open for 13% -> 0% of each run, Pallas kernels for 0% -> 0%
where the time goes in v1:
time: 107 us
  Pallas kernels  97.5 us (91%)
  local copies, waits for them, and re-layouts  7.89 us (7%)
  between operations  1.29 us (1%)
    pallas_call x1, Pallas kernels, body(): pl.pallas_call(functools.partial(kernel, n), out_shape=(jax.ShapeDtypeStr...  97.5 us
    unnamed x9, local copies, waits for them, and re-layouts  7.89 us

profile of v1, /device:TPU:0, one launch (start us, length us, event | category | flops | bytes accessed | tf_op | source)
XLA Modules:
  0.0 106.7 jit_solution(2324319443075798243)
XLA Ops:
  1.3 97.5 %shard_map.137 = (bf16[384,256]{1,0:T(8,128)(2,1)}, bf16[1536,256]{1,0:T(8,128)(2,1)}, bf16[2048,512]{1,0:T(8,128)(2,1)}, f32[1,512]{1,0:T(1,128)}, f32[1,512]{1,0:T(1,128)}) custom-call(bf16[1536,256]{1,0:T(8,128)(2,1)} %fine.1, bf16[8,256,512]{2,1,0:T(8,128)(2,1)} %wd_hbm.1, f32[1,512]{1,0:T(1,128)} %bitcast.8, f32[1,512]{1,0:T(1,128)} %bitcast.9, ...), custom_call_target="tpu_custom_call" | custom-call | tf_op jit(solution)/shard_map/pallas_call | solution.py:319
  98.8 1.6 %copy.21 = bf16[384,256]{1,0:T(8,128)(2,1)} copy(bf16[384,256]{1,0:T(8,128)(2,1)} %get-tuple-element.20) | data formatting | bytes 393216
  100.4 2.1 %copy.22 = bf16[1536,256]{1,0:T(8,128)(2,1)} copy(bf16[1536,256]{1,0:T(8,128)(2,1)} %get-tuple-element.21) | data formatting | bytes 1572864
  102.5 0.0 copy-start.1
  102.5 0.0 copy-start
  102.5 3.0 %copy.23 = bf16[8,256,512]{2,1,0:T(8,128)(2,1)} copy(bf16[8,256,512]{2,1,0:T(8,128)(2,1)} %bitcast.5) | data formatting | bytes 4194304
  105.5 0.0 copy-done.1
  105.5 0.6 copy.24
  106.1 0.0 copy-done
  106.1 0.6 copy.25
Async XLA Ops:
  102.5 3.1 %copy-start.1 = (f32[1,512]{1,0:T(1,128)S(1)}, f32[1,512]{1,0:T(1,128)}, u32[]{:S(2)}) copy-start(f32[1,512]{1,0:T(1,128)} %get-tuple-element.13) | copy-start | bytes 6148
  102.5 3.6 %copy-start = (f32[1,512]{1,0:T(1,128)S(1)}, f32[1,512]{1,0:T(1,128)}, u32[]{:S(2)}) copy-start(f32[1,512]{1,0:T(1,128)} %get-tuple-element.14) | copy-start | bytes 6148

commit v2 on v1

--- a/solution.py
+++ b/solution.py
@@ -9,7 +9,7 @@
 
 OFFSETS = (1, 2, -1, -2)
 EPSILON = 1e-05
-LANES = 2
+LANES = 4
 F32 = jnp.float32
 BF16 = jnp.bfloat16
 MESH = pl.DeviceIdType.MESH
@@ -41,9 +41,9 @@
 def kernel(
     n, fine, wd_hbm, gain, shift, ws_hbm, child, live, send_rows, nbr, gout,
     feat_o, fine_o, down_o, gain_o, shift_o,
-    wd, ws, gath, conv, table, tgrad, facc, gpre, dspread, part,
+    wd, ws, gsend, gpair, conv, table, tgrad, facc, gpre, gppair, crow, dspread, part,
     sbuf, rbuf, obuf, st1, st2, hsend, hrecv, bsend, brecv,
-    wsem, s1s, s1r, s2s, s2r, hss, hsr, bss, bsr, rss, rsr, ags, agr,
+    wsem, pss, psr, s1s, s1r, s2s, s2r, hss, hsr, bss, bsr, rss, rsr, ags, agr,
 ):
     kd, cin, c = wd.shape
     ks, _, co = ws.shape
@@ -51,8 +51,10 @@
     ndir, halo = send_rows.shape
     fine_rows = fine.shape[0]
     ext = rows + ndir * halo
-    q_count, total, width = part.shape
+    q_count, half, width = part.shape
     me = lax.axis_index("coarse")
+    core = lax.rem(me, 2)
+    pair = me + 1 - 2 * core
 
     wd_copy = pltpu.make_async_copy(wd_hbm, wd, wsem.at[0])
     ws_copy = pltpu.make_async_copy(ws_hbm, ws, wsem.at[1])
@@ -85,12 +87,23 @@
     conv[...] = jnp.zeros_like(conv)
     wd_copy.wait()
 
-    @pl.loop(0, kd)
-    def _(k):
+    kh = kd // 2
+
+    def children(k):
         sel = pick_rows(as_column(child[pl.ds(k, 1), :]), fine_rows)
-        g = dot(sel, fine[...]).astype(BF16)
-        gath[k] = g
-        conv[...] += dot(g, wd[k])
+        return dot(sel, fine[...]).astype(BF16)
+
+    @pl.loop(0, kh)
+    def _(i):
+        mine, other = core * kh + i, (1 - core) * kh + i
+        g_other = children(other)
+        gsend[i] = g_other
+        g_mine = children(mine)
+        gpair[i, :rows, :] = g_mine
+        conv[...] += dot(g_other, wd[other]) + dot(g_mine, wd[mine])
+
+    for k in range(kd):
+        crow[:, k * rows : (k + 1) * rows] = child[k : k + 1, :]
 
     wide = conv[...].astype(BF16).astype(F32)
     conv[...] = wide
@@ -106,6 +119,8 @@
     st1[me, 2 * pieces : 2 * pieces + 8, :] = live_count
     pl.semaphore_wait(barrier, n - 1)
     tell_all(st1, s1s, s1r)
+    gath_copy = remote(gsend, gpair.at[:, pl.ds(rows, rows)], pss.at[0], psr.at[0], pair)
+    gath_copy.start()
 
     tgrad[...] = jnp.zeros_like(tgrad)
     ws_copy.wait()
@@ -189,10 +204,14 @@
     def forward(first, last):
         @pl.loop(first, last)
         def _(k):
-            sel = pick_rows(as_column(nbr[pl.ds(k, 1), :]), ext)
-            facc[...] += dot(dot(sel, table[...]).astype(BF16), ws[k])
-
-    forward(0, 3)
+            term = None
+            for i in range(3):
+                sel = pick_rows(as_column(nbr[pl.ds(3 * k + i, 1), :]), ext)
+                term_i = dot(dot(sel, table[...]).astype(BF16), ws[3 * k + i])
+                term = term_i if term is None else term + term_i
+            facc[...] += term
+
+    forward(0, 2)
 
     hear_all(st2, s2s, s2r)
     acc2 = add_slots(st2)
@@ -200,17 +219,34 @@
     grad_shift = flat(acc2, pieces)
     gain_o[...] = grad_gain
     shift_o[...] = grad_shift
-    gpre[...] = (
+    pre = (
         row_mask * gain[...] * inv_std
         * (tgrad[:rows, :] - (grad_shift + conv[...] * grad_gain) / filled)
     ).astype(BF16)
+    gpre[...] = pre
+    gppair[:rows, :] = pre
+    gpre_copy = remote(gpre, gppair.at[pl.ds(rows, rows)], pss.at[1], psr.at[1], pair)
+    gpre_copy.start()
+
+    def spread_down():
+        @pl.loop(0, kd // 4)
+        def _(k4):
+            for i in range(4):
+                k = 4 * k4 + i
+                dspread[pl.ds(pl.multiple_of(k * rows, rows), rows), :] = dot(
+                    gpre[...], wd[k], 1, 1
+                ).astype(BF16)
+
+    spread_down()
+    gath_copy.wait()
+    gpre_copy.wait()
 
     masks = []
-    while 2 ** len(masks) < n:
-        masks.append(2 ** len(masks))
+    while 2 ** (len(masks) + 1) < n:
+        masks.append(2 ** (len(masks) + 1))
     steps = len(masks)
     lows, sends, partners, lengths, places = [], [], [], [], []
-    low, length, place = 0, total, 0
+    low, length, place = 0, half, 0
     for m in masks:
         bit = lax.rem(me // m, 2)
         length = length // 2
@@ -221,6 +257,8 @@
         partners.append(me + m - 2 * m * bit)
         places.append(place)
         place += length
+    base = pl.multiple_of(core * half, half)
+    stages = 2 * steps + 1
 
     def sum_copy(q, s):
         span = pl.ds(places[s], lengths[s])
@@ -228,10 +266,15 @@
             sbuf.at[q, span], rbuf.at[q, span], rss.at[q, s], rsr.at[q, s], partners[s]
         )
 
-    def full_copy(q, s):
-        span = pl.ds(lows[s], lengths[s])
+    def full_copy(q, t):
+        s = 2 * steps - 1 - t
+        if s >= 0:
+            span = pl.ds(pl.multiple_of(base + lows[s], lengths[s]), lengths[s])
+            to = partners[s]
+        else:
+            span, to = pl.ds(base, half), pair
         return remote(
-            obuf.at[q, span], obuf.at[q, span], ags.at[q, s], agr.at[q, s], partners[s]
+            obuf.at[q, span], obuf.at[q, span], ags.at[q, s + 1], agr.at[q, s + 1], to
         )
 
     def start(q, t):
@@ -240,8 +283,8 @@
                 q, pl.ds(sends[t], lengths[t]), :
             ].astype(BF16)
             sum_copy(q, t).start()
-        elif t < 2 * steps:
-            full_copy(q, 2 * steps - 1 - t).start()
+        elif t < stages:
+            full_copy(q, t).start()
 
     def finish(q, t):
         if t < steps:
@@ -251,43 +294,35 @@
             if t < steps - 1:
                 part[q, span, :] = summed
             else:
-                obuf[q, span, :] = summed.astype(BF16)
+                place_o = pl.ds(pl.multiple_of(base + lows[t], lengths[t]), lengths[t])
+                obuf[q, place_o, :] = summed.astype(BF16)
         else:
-            full_copy(q, 2 * steps - 1 - t).wait()
+            full_copy(q, t).wait()
+
+    @pl.loop(0, kh)
+    def _(i):
+        term = dot(gpair[i], gppair[...], 0, 0)
+        for q in range(q_count):
+            part[q, pl.ds(pl.multiple_of(i * cin, cin), cin), :] = term[
+                :, q * width : (q + 1) * width
+            ]
 
     for q in range(q_count):
-        @pl.loop(0, kd)
-        def _(k):
-            part[q, pl.ds(pl.multiple_of(k * cin, cin), cin), :] = dot(
-                gath[k], gpre[:, q * width : (q + 1) * width], 0, 0
-            )
-
         start(q, 0)
-
-    def spread_down():
-        @pl.loop(0, kd)
-        def _(k):
-            dspread[pl.ds(pl.multiple_of(k * rows, rows), rows), :] = dot(
-                gpre[...], wd[k], 1, 1
-            ).astype(BF16)
 
     tile = 256
 
     def fine_tiles(first, last):
         @pl.loop(first, last)
         def _(i):
-            base = pl.multiple_of(i * tile, tile)
-            acc = jnp.zeros((tile, cin), F32)
-            for k in range(kd):
-                sel = drop_rows(child[k : k + 1, :] - base, tile)
-                acc = acc + dot(sel, dspread[k * rows : (k + 1) * rows, :])
-            fine_o[pl.ds(base, tile), :] = acc.astype(BF16)
-
-    units = [functools.partial(forward, k, min(k + 2, ks)) for k in range(3, ks, 2)]
-    units.append(spread_down)
+            first_row = pl.multiple_of(i * tile, tile)
+            sel = drop_rows(crow[...] - first_row, tile)
+            fine_o[pl.ds(first_row, tile), :] = dot(sel, dspread[...]).astype(BF16)
+
+    units = [functools.partial(forward, k, k + 1) for k in range(2, ks // 3)]
     tiles = fine_rows // tile
     units += [functools.partial(fine_tiles, i, i + 1) for i in range(tiles)]
-    for t in range(2 * steps):
+    for t in range(stages):
         for q in range(q_count):
             finish(q, t)
             start(q, t + 1)
@@ -300,6 +335,29 @@
         down_o[:, q * width : (q + 1) * width] = obuf[q]
 
 
+def copies(*refs):
+    count = (len(refs) - 1) // 2
+    sem = refs[-1]
+    moves = [
+        pltpu.make_async_copy(refs[i], refs[count + i], sem.at[i]) for i in range(count)
+    ]
+    for move in moves:
+        move.start()
+    for move in moves:
+        move.wait()
+
+
+def hand_over(*arrays):
+    hbm = pl.BlockSpec(memory_space=pl.ANY)
+    return pl.pallas_call(
+        copies,
+        out_shape=tuple(jax.ShapeDtypeStruct(a.shape, a.dtype) for a in arrays),
+        in_specs=[hbm] * len(arrays),
+        out_specs=(hbm,) * len(arrays),
+        scratch_shapes=[pltpu.SemaphoreType.DMA((len(arrays),))],
+    )(*arrays)
+
+
 def body(fine_feats, down_weight, gain, shift, subm_weight, child, live, send_rows, nbr, grad_out):
     n = lax.axis_size("coarse")
     fine_rows, cin = fine_feats.shape
@@ -310,7 +368,8 @@
     ext = rows + ndir * halo
     width = c // LANES
     total = kd * cin
-    steps = max(1, (n - 1).bit_length())
+    half = total // 2
+    steps = (n - 1).bit_length()
     slot = 2 * (c // 128)
     vmem = pl.BlockSpec(memory_space=pltpu.VMEM)
     hbm = pl.BlockSpec(memory_space=pl.ANY)
@@ -330,16 +389,19 @@
         scratch_shapes=[
             pltpu.VMEM((kd, cin, c), BF16),
             pltpu.VMEM((ks, c, co), BF16),
-            pltpu.VMEM((kd, rows, cin), BF16),
+            pltpu.VMEM((kd // 2, rows, cin), BF16),
+            pltpu.VMEM((kd // 2, 2 * rows, cin), BF16),
             pltpu.VMEM((rows, c), F32),
             pltpu.VMEM((ext, c), BF16),
             pltpu.VMEM((ext, c), F32),
             pltpu.VMEM((rows, co), F32),
             pltpu.VMEM((rows, c), BF16),
+            pltpu.VMEM((2 * rows, c), BF16),
+            pltpu.VMEM((1, kd * rows), jnp.int32),
             pltpu.VMEM((kd * rows, cin), BF16),
-            pltpu.VMEM((LANES, total, width), F32),
-            pltpu.VMEM((LANES, total, width), BF16),
-            pltpu.VMEM((LANES, total, width), BF16),
+            pltpu.VMEM((LANES, half, width), F32),
+            pltpu.VMEM((LANES, half, width), BF16),
+            pltpu.VMEM((LANES, half, width), BF16),
             pltpu.VMEM((LANES, total, width), BF16),
             pltpu.VMEM((n, slot + 8, 128), F32),
             pltpu.VMEM((n, slot, 128), F32),
@@ -347,7 +409,7 @@
             pltpu.VMEM((ndir, halo, c), BF16),
             pltpu.VMEM((ndir, halo, c), BF16),
             pltpu.VMEM((ndir, halo, c), BF16),
-            dma((2,)),
+            dma((2,)), dma((2,)), dma((2,)),
             dma((n,)), dma((n,)), dma((n,)), dma((n,)),
             dma((ndir,)), dma((ndir,)), dma((ndir,)), dma((ndir,)),
             dma((LANES, steps)), dma((LANES, steps)), dma((LANES, steps)), dma((LANES, steps)),
@@ -359,6 +421,7 @@
         fine_feats, down_weight, gain.reshape(1, c), shift.reshape(1, c), subm_weight,
         child, live, send_rows, nbr, grad_out,
     )
+    features, grad_fine, grad_down = hand_over(features, grad_fine, grad_down)
     return (
         features,
         grad_fine,

time: 107 us -> 187 us (1.75)
  Pallas kernels: 97.5 us -> 185 us
  local copies, waits for them, and re-layouts: 7.89 us -> 1.17 us
    pallas_call x0 -> x1, Pallas kernels: none -> 94.4 us  [hand_over(): pl.pallas_call(copies, out_shape=tuple((jax.ShapeDtypeStruct(a.shape, a.d...]
    pallas_call x1, Pallas kernels: 97.5 us -> 90.3 us  [body(): pl.pallas_call(functools.partial(kernel, n), out_shape=(jax.ShapeDtypeStr...]
    unnamed x9 -> x6, local copies, waits for them, and re-layouts: 7.89 us -> 1.17 us
where the time goes in v2:
time: 187 us
  Pallas kernels  185 us (99%)
    pallas_call x1, Pallas kernels, hand_over(): pl.pallas_call(copies, out_shape=tuple((jax.ShapeDtypeStruct(a.shape, a.d...  94.4 us
    pallas_call x1, Pallas kernels, body(): pl.pallas_call(functools.partial(kernel, n), out_shape=(jax.ShapeDtypeStr...  90.3 us

profile of v2, /device:TPU:0, one launch (start us, length us, event | category | flops | bytes accessed | tf_op | source)
XLA Modules:
  0.0 187.2 jit_solution(260134253133679531)
XLA Ops:
  1.3 90.3 %shard_map.137 = (bf16[384,256]{1,0:T(8,128)(2,1)}, bf16[1536,256]{1,0:T(8,128)(2,1)}, bf16[2048,512]{1,0:T(8,128)(2,1)}, f32[1,512]{1,0:T(1,128)}, f32[1,512]{1,0:T(1,128)}) custom-call(bf16[1536,256]{1,0:T(8,128)(2,1)} %fine.1, bf16[8,256,512]{2,1,0:T(8,128)(2,1)} %wd_hbm.1, f32[1,512]{1,0:T(1,128)} %bitcast.7, f32[1,512]{1,0:T(1,128)} %bitcast.8, ...), custom_call_target="tpu_custom_call" | custom-call | tf_op jit(solution)/shard_map/pallas_call | solution.py:378
  91.6 0.0 copy-start.1
  91.6 0.0 copy-start
  91.6 94.4 %shard_map.138 = (bf16[384,256]{1,0:T(8,128)(2,1)}, bf16[1536,256]{1,0:T(8,128)(2,1)}, bf16[2048,512]{1,0:T(8,128)(2,1)}) custom-call(bf16[384,256]{1,0:T(8,128)(2,1)} %get-tuple-element.13.refs_0_, bf16[1536,256]{1,0:T(8,128)(2,1)} %get-tuple-element.14.refs_1_, bf16[2048,512]{1,0:T(8,128)(2,1)} %get-tuple-element.15.refs_2_), custom_call_target="tpu_custom_call" | custom-call | tf_op jit(solution)/shard_map/pallas_call | solution.py:352
  186.0 0.0 copy-done.1
  186.1 0.6 copy.18
  186.6 0.0 copy-done
  186.6 0.6 copy.19
Async XLA Ops:
  91.6 94.5 %copy-start.1 = (f32[1,512]{1,0:T(1,128)S(1)}, f32[1,512]{1,0:T(1,128)}, u32[]{:S(2)}) copy-start(f32[1,512]{1,0:T(1,128)} %get-tuple-element.19) | copy-start | bytes 6148
  91.6 95.0 %copy-start = (f32[1,512]{1,0:T(1,128)S(1)}, f32[1,512]{1,0:T(1,128)}, u32[]{:S(2)}) copy-start(f32[1,512]{1,0:T(1,128)} %get-tuple-element.20) | copy-start | bytes 6148

commit v3 on v2

--- a/solution.py
+++ b/solution.py
@@ -322,39 +322,35 @@
     units = [functools.partial(forward, k, k + 1) for k in range(2, ks // 3)]
     tiles = fine_rows // tile
     units += [functools.partial(fine_tiles, i, i + 1) for i in range(tiles)]
-    for t in range(stages):
-        for q in range(q_count):
-            finish(q, t)
-            start(q, t + 1)
-            if units:
-                units.pop(0)()
-    for unit in units:
-        unit()
+    events = stages * q_count
+    done = 0
+    for event in range(events):
+        t, q = event // q_count, event % q_count
+        finish(q, t)
+        start(q, t + 1)
+        due = (event + 1) * len(units) // events
+        for unit in units[done:due]:
+            unit()
+        done = due
     feat_o[...] = facc[...].astype(BF16)
     for q in range(q_count):
         down_o[:, q * width : (q + 1) * width] = obuf[q]
 
 
 def copies(*refs):
-    count = (len(refs) - 1) // 2
-    sem = refs[-1]
-    moves = [
-        pltpu.make_async_copy(refs[i], refs[count + i], sem.at[i]) for i in range(count)
-    ]
-    for move in moves:
-        move.start()
-    for move in moves:
-        move.wait()
-
-
-def hand_over(*arrays):
-    hbm = pl.BlockSpec(memory_space=pl.ANY)
+    count = len(refs) // 2
+    for i in range(count):
+        refs[count + i][...] = refs[i][...]
+
+
+def hand_over(parts, *arrays):
+    specs = [pl.BlockSpec((a.shape[0] // parts, a.shape[1]), lambda i: (i, 0)) for a in arrays]
     return pl.pallas_call(
         copies,
+        grid=(parts,),
         out_shape=tuple(jax.ShapeDtypeStruct(a.shape, a.dtype) for a in arrays),
-        in_specs=[hbm] * len(arrays),
-        out_specs=(hbm,) * len(arrays),
-        scratch_shapes=[pltpu.SemaphoreType.DMA((len(arrays),))],
+        in_specs=specs,
+        out_specs=tuple(specs),
     )(*arrays)
 
 
@@ -421,7 +417,7 @@
         fine_feats, down_weight, gain.reshape(1, c), shift.reshape(1, c), subm_weight,
         child, live, send_rows, nbr, grad_out,
     )
-    features, grad_fine, grad_down = hand_over(features, grad_fine, grad_down)
+    features, grad_fine, grad_down = hand_over(4, features, grad_fine, grad_down)
     return (
         features,
         grad_fine,

time: 187 us -> 97.6 us (0.52)
  Pallas kernels: 185 us -> 94.9 us
    pallas_call x1, Pallas kernels: 94.4 us -> 4.21 us  [hand_over(): pl.pallas_call(copies, grid=(parts,), out_shape=tuple((jax.ShapeDtypeStru...]
where the time goes in v3:
time: 97.6 us; the launch traced here: 97.4 us
  Pallas kernels  94.9 us (97%)
  between operations  1.31 us (1%)
  local copies, waits for them, and re-layouts  1.17 us (1%)
    pallas_call x1, Pallas kernels, body(): pl.pallas_call(functools.partial(kernel, n), out_shape=(jax.ShapeDtypeStr...  90.7 us
    pallas_call x1, Pallas kernels, hand_over(): pl.pallas_call(copies, grid=(parts,), out_shape=tuple((jax.ShapeDtypeStru...  4.21 us

profile of v3, /device:TPU:0, one launch (start us, length us, event | category | flops | bytes accessed | tf_op | source)
XLA Modules:
  0.0 97.4 jit_solution(11754003147694122388)
XLA Ops:
  1.3 90.7 %shard_map.137 = (bf16[384,256]{1,0:T(8,128)(2,1)}, bf16[1536,256]{1,0:T(8,128)(2,1)}, bf16[2048,512]{1,0:T(8,128)(2,1)}, f32[1,512]{1,0:T(1,128)}, f32[1,512]{1,0:T(1,128)}) custom-call(bf16[1536,256]{1,0:T(8,128)(2,1)} %fine.1, bf16[8,256,512]{2,1,0:T(8,128)(2,1)} %wd_hbm.1, f32[1,512]{1,0:T(1,128)} %bitcast.7, f32[1,512]{1,0:T(1,128)} %bitcast.8, ...), custom_call_target="tpu_custom_call" | custom-call | tf_op jit(solution)/shard_map/pallas_call | solution.py:374
  92.0 0.0 copy-start.1
  92.0 0.0 copy-start
  92.0 4.2 %shard_map.138 = (bf16[384,256]{1,0:T(8,128)(2,1)}, bf16[1536,256]{1,0:T(8,128)(2,1)}, bf16[2048,512]{1,0:T(8,128)(2,1)}) custom-call(bf16[384,256]{1,0:T(8,128)(2,1)} %get-tuple-element.13.refs_0_, bf16[1536,256]{1,0:T(8,128)(2,1)} %get-tuple-element.14.refs_1_, bf16[2048,512]{1,0:T(8,128)(2,1)} %get-tuple-element.15.refs_2_), custom_call_target="tpu_custom_call" | custom-call | tf_op jit(solution)/shard_map/pallas_call | solution.py:348
  96.2 0.0 copy-done.1
  96.2 0.6 copy.18
  96.8 0.0 copy-done
  96.8 0.6 copy.19
Async XLA Ops:
  92.0 4.2 %copy-start.1 = (f32[1,512]{1,0:T(1,128)S(1)}, f32[1,512]{1,0:T(1,128)}, u32[]{:S(2)}) copy-start(f32[1,512]{1,0:T(1,128)} %get-tuple-element.19) | copy-start | bytes 6148
  92.0 4.8 %copy-start = (f32[1,512]{1,0:T(1,128)S(1)}, f32[1,512]{1,0:T(1,128)}, u32[]{:S(2)}) copy-start(f32[1,512]{1,0:T(1,128)} %get-tuple-element.20) | copy-start | bytes 6148
